TPU v7x, 32 devices: a whole 2x2x4 slice. The times are simulated.
32 devices in a mesh: event: 2 (over core), dom: 16 (over z, y, x).
Axes of the slice: x: 2, y: 2, z: 4, core: 2. Of those that a mesh axis runs over, the one named last changes fastest.
Arguments:
- kernels: bfloat16 [4, 16, 64, 125, 128], P('event', 'dom'), may hold values from -12 to 12
- counts: int32 [4, 16, 64, 128], P('event', 'dom'), may hold values from 0 to 3
- volume: bfloat16 [16, 64, 128], P('dom', 'event'), may hold values from 0.29882812 to 3
- tables: bfloat16 [32, 128, 128], replicated, may hold values from 0.049804688 to 1
- pair_offset: int32 [16, 2, 32, 16], P('dom', 'event'), may hold values from 0 to 64, as said below
- pair_table: int32 [16, 2, 32, 16], P('dom', 'event'), may hold values from 0 to 31
Outputs:
- smoothed: bfloat16 [16, 64, 125, 128], P('dom', 'event')
Inputs may be any that keep to these rules, and one draw needn't show every extreme that they name: `pair_offset`: for each block of a device the 16 offsets are distinct and the first is 32.
All inputs are finite; a program needn't handle non-finite values.
Results may differ from a plain program's by a relative error of at most 0.0075.
Values may be sent and summed in bfloat16 or wider, within the bound.
A program may use at most 64 MiB of HBM per device.

v0:
```python
import jax
import jax.numpy as jnp
from jax import lax
from jax.sharding import PartitionSpec as P

EV_DEV = 2
PB = 16


def passed_along(value, axis, steps):
    count = lax.axis_size(axis)
    first, last = (max(0, -steps), min(count, count - steps))
    return lax.ppermute(value, axis, [(source, source + steps) for source in range(first, last)])


def per_device(kernels, counts, volume, tables, pair_offset, pair_table):
    owned = volume.shape[1]
    groups = lax.axis_size("event")
    points = kernels.shape[3]
    width = kernels.shape[4]
    moved, moved_counts = (
        lax.all_to_all(kernels, "event", split_axis=2, concat_axis=0, tiled=True),
        lax.all_to_all(
            counts.astype(jnp.bfloat16), "event", split_axis=2, concat_axis=0, tiled=True
        ),
    )
    grouped = moved.reshape(groups, EV_DEV, owned, points, width)
    partial_value = jnp.sum(grouped, axis=1, dtype=jnp.float32).astype(jnp.bfloat16)
    summed = jnp.sum(partial_value, axis=0, dtype=jnp.float32)
    hits = jnp.sum(moved_counts, axis=0, dtype=jnp.float32)[0]
    vol_rows = volume[0]
    weighted = (
        summed * vol_rows.astype(jnp.float32)[:, None, :] / jnp.sqrt(1.0 + hits)[:, None, :]
    ).astype(jnp.bfloat16)
    source = jnp.concatenate([weighted, vol_rows[:, None, :]], axis=1)
    offsets = pair_offset[0, 0]
    table_ids = pair_table[0, 0]
    places = jnp.arange(owned, dtype=jnp.int32)

    def add_pairs(extended, which):
        matrices = tables[table_ids[:, which]]
        contrib = jnp.einsum("bgs,bst->bgt", source, matrices, preferred_element_type=jnp.float32)
        targets = places + offsets[:, which]
        return (extended.at[targets].add(contrib), None)

    start_buffer = jnp.zeros((3 * owned, points + 1, width), jnp.float32)
    extended, unused = lax.scan(add_pairs, start_buffer, jnp.arange(PB, dtype=jnp.int32))
    from_next = passed_along(extended[:owned].astype(jnp.bfloat16), "dom", -1).astype(jnp.float32)
    from_prev = passed_along(extended[2 * owned :].astype(jnp.bfloat16), "dom", 1).astype(
        jnp.float32
    )
    accumulated = extended[owned : 2 * owned] + from_next + from_prev
    result = accumulated[:, :points] / accumulated[:, points : points + 1]
    return result.astype(jnp.bfloat16)[None]


def solution(mesh):
    in_specs = (
        P("event", "dom", None, None, None),
        P("event", "dom", None, None),
        P("dom", "event", None),
        P(),
        P("dom", "event", None, None),
        P("dom", "event", None, None),
    )
    out_specs = P("dom", "event", None, None)
    return jax.shard_map(
        per_device, mesh=mesh, in_specs=in_specs, out_specs=out_specs, check_vma=False
    )
```

profile of v0, /device:TPU:8, one launch (start us, length us, event | category | flops | bytes accessed | tf_op | source)
XLA Modules:
  0.0 341.5 jit_solution(5359686033963144691)
XLA Ops:
  1.5 3.3 all-to-all-start.1
  5.5 6.8 %copy.34 = bf16[2,1,64,125,128]{4,3,1,0,2:T(8,128)(2,1)} copy(bf16[2,1,64,125,128]{4,2,3,1,0:T(8,128)(2,1)} %param.8) | data formatting | bytes 8192000 | tf_op args[0]
  12.3 5.8 %all-to-all-start = ((bf16[2,1,64,125,128]{4,3,1,0,2:T(8,128)(2,1)}), bf16[2,1,64,125,128]{4,3,1,0,2:T(8,128)(2,1)}, u32[]{:S(2)}, u32[]{:S(2)}) async-start(bf16[2,1,64,125,128]{4,3,1,0,2:T(8,128)(2,1)} %copy.34), calls=%async_computation | async-start | bytes 8388608 | tf_op jit(solution)/shard_map/all_to_all | solution.py:22
  18.2 4.3 %all-to-all-done = bf16[2,1,64,125,128]{4,3,1,0,2:T(8,128)(2,1)} async-done(((bf16[2,1,64,125,128]{4,3,1,0,2:T(8,128)(2,1)}), bf16[2,1,64,125,128]{4,3,1,0,2:T(8,128)(2,1)}, u32[]{:S(2)}, u32[]{:S(2)}) %all-to-all-start) | async-done | bytes 4096032 | tf_op jit(solution)/shard_map/all_to_all | solution.py:22
  22.5 3.4 reduce_sum.37
  28.9 3.4 %broadcast_in_dim.4 = f32[96,126,128]{2,1,0:T(8,128)} broadcast(f32[]{:T(128)} %constant.6.clone.1), dimensions={} | broadcast | bytes 6193156 | tf_op jit(solution)/shard_map/broadcast_in_dim | solution.py:46
  32.4 250.8 %while.11 = (s32[]{:T(128)}, f32[96,126,128]{2,1,0:T(8,128)}, s32[16]{0:T(128)S(1)}, s32[32,16]{0,1:T(8,128)}, s32[32,16]{0,1:T(8,128)}, /*index=5*/bf16[32,128,...) while((s32[]{:T(128)}, f32[96,126,128]{2,1,0:T(8,128)}, ...), condition=%wide.region_6.7_spmd.clone, body=%wide.region_4.6_spmd.clone.sunk | while | flops 132637920 | bytes 16569375 | solution.py:47
  37.6 2.2 convolution_bitcast_fusion.2
  39.8 2.0 copy.45
  41.9 6.3 %scatter_fusion = f32[96,126,128]{2,1,0:T(8,128)} fusion(f32[96,126,128]{2,1,0:T(8,128)} %get-tuple-element.156, s32[32]{0:T(128)S(1)} %get-tuple-element.143, f32[32,126,128]{2,1,0:T(8,128)S(1)} %copy.45), kind=kCustom, calls=%fused_computation.1.clone.clone.1 | custom fusion | flops 516096 | bytes 6193280 | tf_op jit(solution)/shard_map/while/body/eval_jaxpr/scatter-add | solution.py:44
  51.4 2.0 gather_fusion
  53.3 2.2 convolution_bitcast_fusion.2
  55.6 2.0 copy.45
  57.6 6.2 %scatter_fusion = f32[96,126,128]{2,1,0:T(8,128)} fusion(f32[96,126,128]{2,1,0:T(8,128)} %get-tuple-element.156, s32[32]{0:T(128)S(1)} %get-tuple-element.143, f32[32,126,128]{2,1,0:T(8,128)S(1)} %copy.45), kind=kCustom, calls=%fused_computation.1.clone.clone.1 | custom fusion | flops 516096 | bytes 6193280 | tf_op jit(solution)/shard_map/while/body/eval_jaxpr/scatter-add | solution.py:44
  67.1 2.0 gather_fusion
  69.0 2.2 convolution_bitcast_fusion.2
  71.3 2.0 copy.45
  73.3 6.2 %scatter_fusion = f32[96,126,128]{2,1,0:T(8,128)} fusion(f32[96,126,128]{2,1,0:T(8,128)} %get-tuple-element.156, s32[32]{0:T(128)S(1)} %get-tuple-element.143, f32[32,126,128]{2,1,0:T(8,128)S(1)} %copy.45), kind=kCustom, calls=%fused_computation.1.clone.clone.1 | custom fusion | flops 516096 | bytes 6193280 | tf_op jit(solution)/shard_map/while/body/eval_jaxpr/scatter-add | solution.py:44
  82.7 2.0 gather_fusion
  84.7 2.2 convolution_bitcast_fusion.2
  86.9 2.0 copy.45
  89.0 6.2 %scatter_fusion = f32[96,126,128]{2,1,0:T(8,128)} fusion(f32[96,126,128]{2,1,0:T(8,128)} %get-tuple-element.156, s32[32]{0:T(128)S(1)} %get-tuple-element.143, f32[32,126,128]{2,1,0:T(8,128)S(1)} %copy.45), kind=kCustom, calls=%fused_computation.1.clone.clone.1 | custom fusion | flops 516096 | bytes 6193280 | tf_op jit(solution)/shard_map/while/body/eval_jaxpr/scatter-add | solution.py:44
  98.4 2.0 gather_fusion
  100.3 2.2 convolution_bitcast_fusion.2
  102.6 2.0 copy.45
  104.6 6.2 %scatter_fusion = f32[96,126,128]{2,1,0:T(8,128)} fusion(f32[96,126,128]{2,1,0:T(8,128)} %get-tuple-element.156, s32[32]{0:T(128)S(1)} %get-tuple-element.143, f32[32,126,128]{2,1,0:T(8,128)S(1)} %copy.45), kind=kCustom, calls=%fused_computation.1.clone.clone.1 | custom fusion | flops 516096 | bytes 6193280 | tf_op jit(solution)/shard_map/while/body/eval_jaxpr/scatter-add | solution.py:44
  114.0 2.0 gather_fusion
  116.0 2.2 convolution_bitcast_fusion.2
  118.3 2.0 copy.45
  120.3 6.2 %scatter_fusion = f32[96,126,128]{2,1,0:T(8,128)} fusion(f32[96,126,128]{2,1,0:T(8,128)} %get-tuple-element.156, s32[32]{0:T(128)S(1)} %get-tuple-element.143, f32[32,126,128]{2,1,0:T(8,128)S(1)} %copy.45), kind=kCustom, calls=%fused_computation.1.clone.clone.1 | custom fusion | flops 516096 | bytes 6193280 | tf_op jit(solution)/shard_map/while/body/eval_jaxpr/scatter-add | solution.py:44
  131.7 2.2 convolution_bitcast_fusion.2
  133.9 2.0 copy.45
  135.9 6.1 %scatter_fusion = f32[96,126,128]{2,1,0:T(8,128)} fusion(f32[96,126,128]{2,1,0:T(8,128)} %get-tuple-element.156, s32[32]{0:T(128)S(1)} %get-tuple-element.143, f32[32,126,128]{2,1,0:T(8,128)S(1)} %copy.45), kind=kCustom, calls=%fused_computation.1.clone.clone.1 | custom fusion | flops 516096 | bytes 6193280 | tf_op jit(solution)/shard_map/while/body/eval_jaxpr/scatter-add | solution.py:44
  147.3 2.2 convolution_bitcast_fusion.2
  149.5 2.0 copy.45
  151.5 6.2 %scatter_fusion = f32[96,126,128]{2,1,0:T(8,128)} fusion(f32[96,126,128]{2,1,0:T(8,128)} %get-tuple-element.156, s32[32]{0:T(128)S(1)} %get-tuple-element.143, f32[32,126,128]{2,1,0:T(8,128)S(1)} %copy.45), kind=kCustom, calls=%fused_computation.1.clone.clone.1 | custom fusion | flops 516096 | bytes 6193280 | tf_op jit(solution)/shard_map/while/body/eval_jaxpr/scatter-add | solution.py:44
  163.0 2.2 convolution_bitcast_fusion.2
  165.2 2.0 copy.45
  167.2 6.2 %scatter_fusion = f32[96,126,128]{2,1,0:T(8,128)} fusion(f32[96,126,128]{2,1,0:T(8,128)} %get-tuple-element.156, s32[32]{0:T(128)S(1)} %get-tuple-element.143, f32[32,126,128]{2,1,0:T(8,128)S(1)} %copy.45), kind=kCustom, calls=%fused_computation.1.clone.clone.1 | custom fusion | flops 516096 | bytes 6193280 | tf_op jit(solution)/shard_map/while/body/eval_jaxpr/scatter-add | solution.py:44
  178.6 2.2 convolution_bitcast_fusion.2
  180.8 2.0 copy.45
  182.8 6.1 %scatter_fusion = f32[96,126,128]{2,1,0:T(8,128)} fusion(f32[96,126,128]{2,1,0:T(8,128)} %get-tuple-element.156, s32[32]{0:T(128)S(1)} %get-tuple-element.143, f32[32,126,128]{2,1,0:T(8,128)S(1)} %copy.45), kind=kCustom, calls=%fused_computation.1.clone.clone.1 | custom fusion | flops 516096 | bytes 6193280 | tf_op jit(solution)/shard_map/while/body/eval_jaxpr/scatter-add | solution.py:44
  194.2 2.2 convolution_bitcast_fusion.2
  196.4 2.0 copy.45
  198.5 6.2 %scatter_fusion = f32[96,126,128]{2,1,0:T(8,128)} fusion(f32[96,126,128]{2,1,0:T(8,128)} %get-tuple-element.156, s32[32]{0:T(128)S(1)} %get-tuple-element.143, f32[32,126,128]{2,1,0:T(8,128)S(1)} %copy.45), kind=kCustom, calls=%fused_computation.1.clone.clone.1 | custom fusion | flops 516096 | bytes 6193280 | tf_op jit(solution)/shard_map/while/body/eval_jaxpr/scatter-add | solution.py:44
  210.0 2.2 convolution_bitcast_fusion.2
  212.2 2.0 copy.45
  214.2 6.1 %scatter_fusion = f32[96,126,128]{2,1,0:T(8,128)} fusion(f32[96,126,128]{2,1,0:T(8,128)} %get-tuple-element.156, s32[32]{0:T(128)S(1)} %get-tuple-element.143, f32[32,126,128]{2,1,0:T(8,128)S(1)} %copy.45), kind=kCustom, calls=%fused_computation.1.clone.clone.1 | custom fusion | flops 516096 | bytes 6193280 | tf_op jit(solution)/shard_map/while/body/eval_jaxpr/scatter-add | solution.py:44
  225.6 2.2 convolution_bitcast_fusion.2
  227.8 2.0 copy.45
  229.8 6.2 %scatter_fusion = f32[96,126,128]{2,1,0:T(8,128)} fusion(f32[96,126,128]{2,1,0:T(8,128)} %get-tuple-element.156, s32[32]{0:T(128)S(1)} %get-tuple-element.143, f32[32,126,128]{2,1,0:T(8,128)S(1)} %copy.45), kind=kCustom, calls=%fused_computation.1.clone.clone.1 | custom fusion | flops 516096 | bytes 6193280 | tf_op jit(solution)/shard_map/while/body/eval_jaxpr/scatter-add | solution.py:44
  241.3 2.2 convolution_bitcast_fusion.2
  243.5 2.0 copy.45
  245.5 6.3 %scatter_fusion = f32[96,126,128]{2,1,0:T(8,128)} fusion(f32[96,126,128]{2,1,0:T(8,128)} %get-tuple-element.156, s32[32]{0:T(128)S(1)} %get-tuple-element.143, f32[32,126,128]{2,1,0:T(8,128)S(1)} %copy.45), kind=kCustom, calls=%fused_computation.1.clone.clone.1 | custom fusion | flops 516096 | bytes 6193280 | tf_op jit(solution)/shard_map/while/body/eval_jaxpr/scatter-add | solution.py:44
  257.0 2.2 convolution_bitcast_fusion.2
  259.3 2.0 copy.45
  261.3 6.2 %scatter_fusion = f32[96,126,128]{2,1,0:T(8,128)} fusion(f32[96,126,128]{2,1,0:T(8,128)} %get-tuple-element.156, s32[32]{0:T(128)S(1)} %get-tuple-element.143, f32[32,126,128]{2,1,0:T(8,128)S(1)} %copy.45), kind=kCustom, calls=%fused_computation.1.clone.clone.1 | custom fusion | flops 516096 | bytes 6193280 | tf_op jit(solution)/shard_map/while/body/eval_jaxpr/scatter-add | solution.py:44
  272.8 2.2 convolution_bitcast_fusion.2
  275.0 2.0 copy.45
  277.0 6.2 %scatter_fusion = f32[96,126,128]{2,1,0:T(8,128)} fusion(f32[96,126,128]{2,1,0:T(8,128)} %get-tuple-element.156, s32[32]{0:T(128)S(1)} %get-tuple-element.143, f32[32,126,128]{2,1,0:T(8,128)S(1)} %copy.45), kind=kCustom, calls=%fused_computation.1.clone.clone.1 | custom fusion | flops 516096 | bytes 6193280 | tf_op jit(solution)/shard_map/while/body/eval_jaxpr/scatter-add | solution.py:44
  283.2 6.6 %fusion.7 = (bf16[96,126,128]{2,0,1:T(8,128)(2,1)S(1)}, f32[96,126,128]{2,0,1:T(8,128)S(1)}) fusion(f32[96,126,128]{2,1,0:T(8,128)} %get-tuple-element.47), kind=kLoop, calls=%fused_computation.23 | loop fusion | flops 1548288 | bytes 15482880 | tf_op jit(solution)/shard_map/convert.4
  290.2 4.2 %collective-permute-start = (bf16[32,126,128]{2,0,1:T(8,128)(2,1)S(1)}, bf16[32,126,128]{2,0,1:T(8,128)(2,1)S(1)}, u32[]{:S(2)}, u32[]{:S(2)}) collective-permute-start(bf16[32,126,128]{2,0,1:T(8,128)(2,1)S(1)} %get-tuple-element.96), channel_id=1, source_target_pairs={{1,0},{2,1},{3,2},{4,3},{5,4},{6,5},{7,6},{8,7},{9,8},{10,9},{11,1... | collective-permute-start | bytes 3096584 | tf_op jit(solution)/shard_map/ppermute | solution.py:13
  296.4 21.3 %collective-permute-done = bf16[32,126,128]{2,0,1:T(8,128)(2,1)S(1)} collective-permute-done((bf16[32,126,128]{2,0,1:T(8,128)(2,1)S(1)}, bf16[32,126,128]{2,0,1:T(8,128)(2,1)S(1)}, u32[]{:S(2)}, u32[]{:S(2)}) %collective-permute-start) | collective-permute-done | bytes 1032224 | tf_op jit(solution)/shard_map/ppermute | solution.py:13
  317.7 22.2 %collective-permute-done.1 = bf16[32,126,128]{2,0,1:T(8,128)(2,1)S(1)} collective-permute-done((bf16[32,126,128]{2,0,1:T(8,128)(2,1)S(1)}, bf16[32,126,128]{2,0,1:T(8,128)(2,1)S(1)}, u32[]{:S(2)}, u32[]{:S(2)}) %collective-permute-start.1) | collective-permute-done | bytes 1032224 | tf_op jit(solution)/shard_map/ppermute | solution.py:13
  (78 shorter events, 51.9 us)
Async XLA Ops:
  1.5 10.7 %all-to-all-start.1 = ((bf16[2,1,64,128]{3,0,1,2:T(2,128)(2,1)}), bf16[2,1,64,128]{3,0,1,2:T(2,128)(2,1)S(1)}, u32[]{:S(2)}, u32[]{:S(2)}) async-start(bf16[2,1,64,128]{3,0,1,2:T(2,128)(2,1)} %copy_convert_fusion), calls=%async_computation.1 | async-start | bytes 65536 | tf_op jit(solution)/shard_map/all_to_all | solution.py:23
  12.3 10.2 %all-to-all-start = ((bf16[2,1,64,125,128]{4,3,1,0,2:T(8,128)(2,1)}), bf16[2,1,64,125,128]{4,3,1,0,2:T(8,128)(2,1)}, u32[]{:S(2)}, u32[]{:S(2)}) async-start(bf16[2,1,64,125,128]{4,3,1,0,2:T(8,128)(2,1)} %copy.34), calls=%async_computation | async-start | bytes 8388608 | tf_op jit(solution)/shard_map/all_to_all | solution.py:22
  27.7 0.7 copy-start
  290.2 27.5 %collective-permute-start = (bf16[32,126,128]{2,0,1:T(8,128)(2,1)S(1)}, bf16[32,126,128]{2,0,1:T(8,128)(2,1)S(1)}, u32[]{:S(2)}, u32[]{:S(2)}) collective-permute-start(bf16[32,126,128]{2,0,1:T(8,128)(2,1)S(1)} %get-tuple-element.96), channel_id=1, source_target_pairs={{1,0},{2,1},{3,2},{4,3},{5,4},{6,5},{7,6},{8,7},{9,8},{10,9},{11,1... | collective-permute-start | bytes 3096584 | tf_op jit(solution)/shard_map/ppermute | solution.py:13
  294.4 45.4 %collective-permute-start.1 = (bf16[32,126,128]{2,0,1:T(8,128)(2,1)S(1)}, bf16[32,126,128]{2,0,1:T(8,128)(2,1)S(1)}, u32[]{:S(2)}, u32[]{:S(2)}) collective-permute-start(bf16[32,126,128]{2,0,1:T(8,128)(2,1)S(1)} %get-tuple-element.97), channel_id=1, source_target_pairs={{0,1},{1,2},{2,3},{3,4},{4,5},{5,6},{6,7},{7,8},{8,9},{9,10},{10,1... | collective-permute-start | bytes 3096584 | tf_op jit(solution)/shard_map/ppermute | solution.py:13
where the time goes:
time: 348 us; the launch traced here: 341 us
  other arithmetic  126 us (36%)
  local copies, waits for them, and re-layouts  85.8 us (25%)
  waiting for transfers between devices  47.8 us (14%)
  matrix products  35.6 us (10%)
  loops' own time  31.4 us (9%)
  starting transfers between devices  15.2 us (4%)
    scatter-add x16, other arithmetic, add_pairs(): return (extended.at[targets].add(contrib), None)  99.1 us
    ppermute x2, waiting for transfers between devices, passed_along(): lax.ppermute(value, axis, [(source, source + steps) for source in range(f...  43.5 us
    dot_general x16, matrix products, add_pairs(): jnp.einsum('bgs,bst->bgt', source, matrices, preferred_element_type=jnp.f...  35.6 us
    dot_general x16, local copies, waits for them, and re-layouts, add_pairs(): jnp.einsum('bgs,bst->bgt', source, matrices, preferred_element_type=jnp.f...  32.1 us
    gather x16, local copies, waits for them, and re-layouts, add_pairs(): matrices = tables[table_ids[:, which]]  31.6 us
    another operation x1, loops' own time, per_device(): lax.scan(add_pairs, start_buffer, jnp.arange(PB, dtype=jnp.int32))  31.4 us
    select_n x16, other arithmetic, add_pairs(): return (extended.at[targets].add(contrib), None)  11.5 us
    dynamic_slice x16, local copies, waits for them, and re-layouts, per_device(): lax.scan(add_pairs, start_buffer, jnp.arange(PB, dtype=jnp.int32))  9.31 us
  transfers between devices with their start and end apart: 4, of which 3 were waited for; matrix products, arithmetic and copies ran while one was open for 2% of the time, Pallas kernels for 0%

commit v1 on v0

v1 whole, which is shorter than its diff:
```python
import functools

import jax
import jax.numpy as jnp
from jax import lax
from jax.experimental import pallas as pl
from jax.experimental.pallas import tpu as pltpu
from jax.sharding import PartitionSpec as P

CHUNK = 4
MESH = pl.DeviceIdType.MESH


def kernel(
    sizes,
    kernels, counts, volume, tables, index_smem, index_vmem, out,
    kbuf, part_out, part_in, count_out, count_in, scale, vol, stage,
    source, mate, far, tab, acc, index_mate, index_far, index_mate_s, index_far_s,
    ksem, tsem, csem, xsem, isem, msem, fsem,
):
    n = sizes["dom"]
    events, owned, points, width = sizes["events"], sizes["owned"], sizes["points"], sizes["width"]
    chunks = owned // CHUNK
    core = lax.axis_index("event")
    me = lax.axis_index("dom")
    odd = lax.rem(me, 2)
    step = 2 - 4 * odd
    buddy = (1 - core, me)
    partner = (core, me + 1 - 2 * odd)
    has_out = jnp.logical_and(me + step >= 0, me + step < n)
    has_in = jnp.logical_and(me - step >= 0, me - step < n)
    far_out = (core, jnp.where(has_out, me + step, me - step))
    far_in = (core, jnp.where(has_in, me - step, me + step))

    def fetch(side, c):
        start = (core if side else 1 - core) * owned + c * CHUNK
        return pltpu.make_async_copy(
            kernels.at[:, 0, pl.ds(start, CHUNK)], kbuf.at[side, c], ksem.at[side, c]
        )

    for side in (0, 1):
        for c in range(chunks):
            fetch(side, c).start()
    get_tables = pltpu.make_async_copy(tables, tab.at[pl.ds(1, sizes["tables"])], tsem.at[0])
    get_tables.start()

    barrier = pltpu.get_barrier_semaphore()
    pl.semaphore_signal(barrier, inc=1, device_id=buddy, device_id_type=MESH)
    pl.semaphore_signal(barrier, inc=1, device_id=partner, device_id_type=MESH)

    @pl.when(has_out)
    def _():
        pl.semaphore_signal(barrier, inc=1, device_id=far_out, device_id_type=MESH)

    @pl.when(has_in)
    def _():
        pl.semaphore_signal(barrier, inc=1, device_id=far_in, device_id_type=MESH)

    tab[0] = jnp.zeros((width, width), tab.dtype)
    acc[...] = jnp.zeros_like(acc)
    stage[...] = jnp.zeros_like(stage)
    vol[...] = volume[0].astype(jnp.float32)
    other = pl.multiple_of((1 - core) * owned, owned)
    own = pl.multiple_of(core * owned, owned)
    count_out[...] = sum(counts[e, 0, pl.ds(other, owned)] for e in range(events))
    pl.semaphore_wait(barrier, 2 + has_out.astype(jnp.int32) + has_in.astype(jnp.int32))

    def remote(src, dst, sems, where, device):
        return pltpu.make_async_remote_copy(
            src_ref=src, dst_ref=dst, send_sem=sems.at[(0, *where)], recv_sem=sems.at[(1, *where)],
            device_id=device, device_id_type=MESH,
        )

    send_count = remote(count_out, count_in, csem, (0,), buddy)
    send_index = remote(index_vmem, index_mate, isem, (0,), partner)
    pass_index = remote(index_mate, index_far, isem, (1,), far_out)
    send_part = lambda c: remote(part_out.at[c], part_in.at[c], xsem, (c,), buddy)
    send_source = lambda c: remote(source.at[c], mate.at[c], msem, (c,), partner)
    pass_source = lambda c: remote(mate.at[c], far.at[c], fsem, (c,), far_out)
    send_count.start()
    send_index.start()

    def event_sum(side, c, b):
        total = kbuf[side, c, 0, b].astype(jnp.float32)
        for e in range(1, events):
            total = total + kbuf[side, c, e, b].astype(jnp.float32)
        return total.astype(jnp.bfloat16)

    def give(c, carry):
        fetch(0, c).wait()
        for b in range(CHUNK):
            part_out[c, b] = event_sum(0, c, b)
        send_part(c).start()
        return carry

    lax.fori_loop(0, chunks, give, 0)

    send_count.wait()
    hits = sum(counts[e, 0, pl.ds(own, owned)] for e in range(events)) + count_in[...]
    scale[...] = vol[...] / jnp.sqrt(1.0 + hits.astype(jnp.float32))

    def weigh(c, carry):
        fetch(1, c).wait()
        send_part(c).wait_recv()
        for b in range(CHUNK):
            row = pl.ds(c * CHUNK + b, 1)
            total = event_sum(1, c, b).astype(jnp.float32) + part_in[c, b].astype(jnp.float32)
            stage[b, :points] = total * scale[row]
            stage[b, points : points + 1] = vol[row]
        for b in range(CHUNK):
            source[c, :, b * width : (b + 1) * width] = stage[b].astype(jnp.bfloat16)
        send_source(c).start()
        return carry

    lax.fori_loop(0, chunks, weigh, 0)
    get_tables.wait()

    def multiply(blocks, indices, c, shift, first, last):
        def group(g, carry):
            for h in range(CHUNK // 2):
                pair = g * (CHUNK // 2) + h
                weights = jnp.concatenate(
                    [
                        jnp.concatenate(
                            [tab[indices[c * CHUNK + b, shift + 2 * pair + t]] for t in (0, 1)],
                            axis=1,
                        )
                        for b in range(CHUNK)
                    ],
                    axis=0,
                )
                acc[pair] += jnp.dot(blocks[c], weights, preferred_element_type=jnp.float32)
            return carry

        lax.fori_loop(first, last, group, 0)

    send_index.wait()

    @pl.when(has_out)
    def _():
        pass_index.start()

    to_mate = pltpu.make_async_copy(index_mate, index_mate_s, tsem.at[1])
    to_mate.start()
    to_mate.wait()

    def far_part(c):
        pass_source(c).wait_recv()
        multiply(far, index_far_s, c, 2 * owned * (1 - odd), odd * c, jnp.where(odd == 1, chunks, c + 1))

    def work(c, carry):
        send_source(c).wait_recv()

        @pl.when(has_out)
        def _():
            pass_source(c).start()

        multiply(source, index_smem, c, owned, 0, chunks)
        multiply(mate, index_mate_s, c, 2 * owned * odd, (1 - odd) * c, jnp.where(odd == 1, c + 1, chunks))

        @pl.when(jnp.logical_and(has_in, c == 0))
        def _():
            pass_index.wait_recv()
            to_far = pltpu.make_async_copy(index_far, index_far_s, tsem.at[2])
            to_far.start()
            to_far.wait()

        @pl.when(jnp.logical_and(has_in, c >= 1))
        def _():
            far_part(c - 1)

        return carry

    lax.fori_loop(0, chunks, work, 0)

    @pl.when(has_in)
    def _():
        far_part(chunks - 1)

    def finish(i, carry):
        for t in (0, 1):
            lanes = slice(t * width, (t + 1) * width)
            inverse = 1.0 / acc[i, points : points + 1, lanes]
            out[2 * i + t] = (acc[i, :points, lanes] * inverse).astype(out.dtype)
        return carry

    lax.fori_loop(0, owned // 2, finish, 0)

    def drain(c, carry):
        send_part(c).wait_send()
        send_source(c).wait_send()

        @pl.when(has_out)
        def _():
            pass_source(c).wait_send()

        return carry

    lax.fori_loop(0, chunks, drain, 0)

    @pl.when(has_out)
    def _():
        pass_index.wait_send()


def per_device(kernels, counts, volume, tables, pair_offset, pair_table):
    events, owned = kernels.shape[0], volume.shape[1]
    points, width = kernels.shape[3:]
    rows = -(-(points + 1) // 16) * 16
    chunks = owned // CHUNK
    lanes = -(-3 * owned // 128) * 128
    targets = jnp.arange(owned, dtype=jnp.int32)[:, None] + pair_offset[0, 0]
    here = targets[:, :, None] == jnp.arange(lanes, dtype=jnp.int32)
    index = jnp.sum(jnp.where(here, pair_table[0, 0][:, :, None] + 1, 0), axis=1, dtype=jnp.int32)
    sizes = dict(
        dom=lax.axis_size("dom"), events=events, owned=owned, points=points, width=width,
        tables=tables.shape[0],
    )
    vmem = pl.BlockSpec(memory_space=pltpu.VMEM)
    hbm = pl.BlockSpec(memory_space=pl.ANY)
    dma = pltpu.SemaphoreType.DMA
    bf16, f32, i32 = jnp.bfloat16, jnp.float32, jnp.int32
    blocks = pltpu.VMEM((chunks, rows, CHUNK * width), bf16)
    return pl.pallas_call(
        functools.partial(kernel, sizes),
        out_shape=jax.ShapeDtypeStruct((owned, points, width), bf16),
        in_specs=[hbm, vmem, vmem, hbm, pl.BlockSpec(memory_space=pltpu.SMEM), vmem],
        out_specs=vmem,
        scratch_shapes=[
            pltpu.VMEM((2, chunks, events, CHUNK, points, width), bf16),
            pltpu.VMEM((chunks, CHUNK, points, width), bf16),
            pltpu.VMEM((chunks, CHUNK, points, width), bf16),
            pltpu.VMEM((owned, width), i32),
            pltpu.VMEM((owned, width), i32),
            pltpu.VMEM((owned, width), f32),
            pltpu.VMEM((owned, width), f32),
            pltpu.VMEM((CHUNK, rows, width), f32),
            blocks, blocks, blocks,
            pltpu.VMEM((tables.shape[0] + 1, width, width), bf16),
            pltpu.VMEM((owned // 2, rows, 2 * width), f32),
            pltpu.VMEM((owned, lanes), i32),
            pltpu.VMEM((owned, lanes), i32),
            pltpu.SMEM((owned, lanes), i32),
            pltpu.SMEM((owned, lanes), i32),
            dma((2, chunks)),
            dma((3,)),
            dma((2, 1)),
            dma((2, chunks)),
            dma((2, 2)),
            dma((2, chunks)),
            dma((2, chunks)),
        ],
        compiler_params=pltpu.CompilerParams(
            collective_id=0, has_side_effects=True, vmem_limit_bytes=40 * 2**20
        ),
    )(kernels, counts, volume, tables, index, index)[None]


def solution(mesh):
    in_specs = (
        P("event", "dom", None, None, None),
        P("event", "dom", None, None),
        P("dom", "event", None),
        P(),
        P("dom", "event", None, None),
        P("dom", "event", None, None),
    )
    out_specs = P("dom", "event", None, None)
    return jax.shard_map(
        per_device, mesh=mesh, in_specs=in_specs, out_specs=out_specs, check_vma=False
    )
```

time: 348 us -> 54.5 us (0.16); the launches traced: 341 us -> 54.2 us
  other arithmetic: 126 us -> 1.7 us
  local copies, waits for them, and re-layouts: 85.8 us -> 6.6 us
  waiting for transfers between devices: 47.8 us -> 0 us
  Pallas kernels: 0 us -> 45.8 us
  matrix products: 35.6 us -> 0 us
  loops' own time: 31.4 us -> 0 us
  starting transfers between devices: 15.2 us -> 0 us
    scatter-add x16 -> x0, other arithmetic: 99.1 us -> none  [add_pairs(): return (extended.at[targets].add(contrib), None)]
    pallas_call x0 -> x1, Pallas kernels: none -> 45.8 us  [per_device(): pl.pallas_call(functools.partial(kernel, sizes), out_shape=jax.ShapeDtype...]
    ppermute x2 -> x0, waiting for transfers between devices: 43.5 us -> none  [passed_along(): lax.ppermute(value, axis, [(source, source + steps) for source in range(f...]
    dot_general x16 -> x0, matrix products: 35.6 us -> none  [add_pairs(): jnp.einsum('bgs,bst->bgt', source, matrices, preferred_element_type=jnp.f...]
    dot_general x16 -> x0, local copies, waits for them, and re-layouts: 32.1 us -> none  [add_pairs(): jnp.einsum('bgs,bst->bgt', source, matrices, preferred_element_type=jnp.f...]
    gather x16 -> x0, local copies, waits for them, and re-layouts: 31.6 us -> none  [add_pairs(): matrices = tables[table_ids[:, which]]]
    another operation x1 -> x0, loops' own time: 31.4 us -> none  [per_device(): lax.scan(add_pairs, start_buffer, jnp.arange(PB, dtype=jnp.int32))]
    select_n x16 -> x0, other arithmetic: 11.5 us -> none  [add_pairs(): return (extended.at[targets].add(contrib), None)]
  transfers between devices with their start and end apart: 4 -> 0, of which waited for: 3 -> 0; matrix products, arithmetic and copies ran while one was open for 2% -> 0% of each run, Pallas kernels for 0% -> 0%
where the time goes in v1:
time: 54.5 us; the launch traced here: 54.2 us
  Pallas kernels  45.8 us (84%)
  local copies, waits for them, and re-layouts  6.6 us (12%)
  other arithmetic  1.7 us (3%)
    pallas_call x1, Pallas kernels, per_device(): pl.pallas_call(functools.partial(kernel, sizes), out_shape=jax.ShapeDtype...  45.8 us
    unnamed x7, local copies, waits for them, and re-layouts  4.82 us
    broadcast_in_dim x1, local copies, waits for them, and re-layouts, per_device(): pl.pallas_call(functools.partial(kernel, sizes), out_shape=jax.ShapeDtype...  1.62 us

profile of v1, /device:TPU:8, one launch (start us, length us, event | category | flops | bytes accessed | tf_op | source)
XLA Modules:
  0.0 54.2 jit_solution(16548749622165444193)
XLA Ops:
  0.0 0.7 %bitcast_add_fusion = s32[32,16]{0,1:T(8,128)S(1)} fusion(s32[1,1,32,16]{2,3,1,0:T(8,128)} %param.10), kind=kLoop, calls=%fused_computation.2 | loop fusion | flops 512 | bytes 4096 | tf_op jit(solution)/shard_map/add | solution.py:212
  0.7 0.1 copy.11
  0.8 0.0 copy-start
  0.8 0.0 copy-start.1
  0.8 0.0 copy-start.2
  0.8 0.8 %add_bitcast_fusion = s32[32,16]{0,1:T(8,128)S(1)} fusion(s32[1,1,32,16]{2,3,1,0:T(8,128)} %param.11), kind=kLoop, calls=%fused_computation.3 | loop fusion | flops 512 | bytes 4096 | tf_op jit(solution)/shard_map/add | solution.py:214
  1.6 0.1 copy.12
  1.7 0.2 select_reduce_fusion.index_smem.index_vmem
  1.9 4.8 %copy.13.kernels = bf16[2,1,64,125,128]{4,3,2,1,0:T(8,128)(2,1)S(1)} copy(bf16[2,1,64,125,128]{4,2,3,1,0:T(8,128)(2,1)} %param.6) | data formatting | bytes 8192000 | tf_op args[0]
  6.7 0.0 copy-done
  6.7 0.0 copy-done.1
  6.7 0.0 copy-done.2
  6.7 45.8 %shard_map.64 = bf16[32,125,128]{2,1,0:T(8,128)(2,1)S(1)} custom-call(bf16[2,1,64,125,128]{4,3,2,1,0:T(8,128)(2,1)S(1)} %copy.13.kernels, s32[2,1,64,128]{3,2,1,0:T(8,128)S(1)} %copy-done.1, bf16[1,32,128]{2,1,0:T(8,128)(2,1)S(1)} %copy-done.2, bf16[32,128,128]{2,1,0:T(8,128)(2,1)S(1)} %copy-done, s32[32,128]{1,0:T(8,128)S(1)} %select_reduce_fusion.index_smem.index_vmem, ...), custom_call_target="tpu_custom_call" | custom-call | tf_op jit(solution)/shard_map/pallas_call | solution.py:224
  52.6 1.6 %copy.14 = bf16[1,32,125,128]{3,1,2,0:T(8,128)(2,1)} copy(bf16[1,32,125,128]{3,2,1,0:T(8,128)(2,1)S(1)} %bitcast.5) | data formatting | bytes 2048000 | tf_op jit(solution)/shard_map/broadcast_in_dim | solution.py:224
Async XLA Ops:
  0.8 5.9 %copy-start = (bf16[32,128,128]{2,1,0:T(8,128)(2,1)S(1)}, bf16[32,128,128]{2,1,0:T(8,128)(2,1)}, u32[]{:S(2)}) copy-start(bf16[32,128,128]{2,1,0:T(8,128)(2,1)} %tables.1) | copy-start | bytes 3145732
  0.8 5.9 %copy-start.1 = (s32[2,1,64,128]{3,2,1,0:T(8,128)S(1)}, s32[2,1,64,128]{3,2,1,0:T(8,128)}, u32[]{:S(2)}) copy-start(s32[2,1,64,128]{3,2,1,0:T(8,128)} %counts.1) | copy-start | bytes 196612
  0.8 5.9 %copy-start.2 = (bf16[1,32,128]{2,1,0:T(8,128)(2,1)S(1)}, bf16[1,32,128]{2,1,0:T(8,128)(2,1)}, u32[]{:S(2)}) copy-start(bf16[1,32,128]{2,1,0:T(8,128)(2,1)} %volume.1) | copy-start | bytes 24580

commit v2 on v1

v2 whole, which is shorter than its diff:
```python
import functools

import jax
import jax.numpy as jnp
from jax import lax
from jax.experimental import pallas as pl
from jax.experimental.pallas import tpu as pltpu
from jax.sharding import PartitionSpec as P

UNIT = 2
CHUNK = 8
HALF = 16
MESH = pl.DeviceIdType.MESH


def kernel(
    sizes,
    kernels, counts, volume, tables, index_smem, index_vmem, out,
    kbuf, part_out, part_in, count_out, count_in, stage, result,
    source, mate, far, tab, acc, index_mate, index_far, index_mate_s, index_far_s,
    ksem, tsem, csem, xsem, isem, msem, fsem,
):
    n = sizes["dom"]
    events, owned, points, width = sizes["events"], sizes["owned"], sizes["points"], sizes["width"]
    cut = sizes["cut"]
    rows = stage.shape[0] // HALF
    slabs, halves, units, chunks = points // cut, owned // HALF, owned // UNIT, owned // CHUNK
    core = lax.axis_index("event")
    me = lax.axis_index("dom")
    odd = lax.rem(me, 2)
    step = 2 - 4 * odd
    buddy = (1 - core, me)
    partner = (core, me + 1 - 2 * odd)
    has_out = jnp.logical_and(me + step >= 0, me + step < n)
    has_in = jnp.logical_and(me - step >= 0, me - step < n)
    far_out = (core, jnp.where(has_out, me + step, me - step))
    far_in = (core, jnp.where(has_in, me - step, me + step))

    def fetch(side, h):
        start = pl.multiple_of((core if side else 1 - core) * owned + h * HALF, HALF)
        return pltpu.make_async_copy(
            kernels.at[:, 0, :, pl.ds(start, HALF)], kbuf.at[side, h], ksem.at[side, h]
        )

    for h in range(halves):
        for side in (0, 1):
            fetch(side, h).start()
    get_tables = pltpu.make_async_copy(tables, tab.at[pl.ds(1, sizes["tables"])], tsem.at[0])
    get_tables.start()

    barrier = pltpu.get_barrier_semaphore()
    pl.semaphore_signal(barrier, inc=1, device_id=buddy, device_id_type=MESH)
    pl.semaphore_signal(barrier, inc=1, device_id=partner, device_id_type=MESH)

    @pl.when(has_out)
    def _():
        pl.semaphore_signal(barrier, inc=1, device_id=far_out, device_id_type=MESH)

    @pl.when(has_in)
    def _():
        pl.semaphore_signal(barrier, inc=1, device_id=far_in, device_id_type=MESH)

    tab[0] = jnp.zeros((width, width), tab.dtype)
    acc[...] = jnp.zeros_like(acc)
    stage[(points + 1) * HALF :] = jnp.zeros((stage.shape[0] - (points + 1) * HALF, width), jnp.float32)
    vol = volume[0].astype(jnp.float32)
    other = pl.multiple_of((1 - core) * owned, owned)
    own = pl.multiple_of(core * owned, owned)
    count_out[...] = sum(counts[e, 0, pl.ds(other, owned)] for e in range(events))
    pl.semaphore_wait(barrier, 2 + has_out.astype(jnp.int32) + has_in.astype(jnp.int32))

    def remote(src, dst, sems, where, device):
        return pltpu.make_async_remote_copy(
            src_ref=src, dst_ref=dst, send_sem=sems.at[(0, *where)], recv_sem=sems.at[(1, *where)],
            device_id=device, device_id_type=MESH,
        )

    send_count = remote(count_out, count_in, csem, (0,), buddy)
    send_index = remote(index_vmem, index_mate, isem, (0,), partner)
    pass_index = remote(index_mate, index_far, isem, (1,), far_out)
    send_part = lambda h, q: remote(part_out.at[h, q], part_in.at[h, q], xsem, (h, q), buddy)
    send_source = lambda u: remote(source.at[u], mate.at[u], msem, (u,), partner)
    pass_source = lambda u: remote(mate.at[u], far.at[u], fsem, (u,), far_out)
    send_count.start()
    send_index.start()

    def event_sum(side, h, g):
        total = kbuf[side, h, 0, g].astype(jnp.float32)
        for e in range(1, events):
            total = total + kbuf[side, h, e, g].astype(jnp.float32)
        return total.astype(jnp.bfloat16)

    for h in range(halves):
        fetch(0, h).wait()

        def give(q, carry):
            for r in range(cut):
                part_out[h, q, r] = event_sum(0, h, q * cut + r)
            send_part(h, q).start()
            return carry

        lax.fori_loop(0, slabs, give, 0)

    send_count.wait()
    hits = sum(counts[e, 0, pl.ds(own, owned)] for e in range(events)) + count_in[...]
    scale = vol / jnp.sqrt(1.0 + hits.astype(jnp.float32))

    for h in range(halves):
        fetch(1, h).wait()
        here = slice(h * HALF, (h + 1) * HALF)
        factor = scale[here]

        def weigh(q, carry):
            send_part(h, q).wait_recv()
            for r in range(cut):
                g = q * cut + r
                total = event_sum(1, h, g).astype(jnp.float32) + part_in[h, q, r].astype(jnp.float32)
                stage[pl.ds(pl.multiple_of(g * HALF, HALF), HALF)] = total * factor
            return carry

        lax.fori_loop(0, slabs, weigh, 0)
        stage[points * HALF : (points + 1) * HALF] = vol[here]
        for u in range(HALF // UNIT):
            unit = h * (HALF // UNIT) + u
            for b in range(UNIT):
                block = stage[pl.ds(u * UNIT + b, rows, stride=HALF)]
                source[unit, :, b * width : (b + 1) * width] = block.astype(jnp.bfloat16)
            send_source(unit).start()

    get_tables.wait()

    def multiply(blocks, indices, c, shift, first, last):
        left = jnp.concatenate([blocks[c * (CHUNK // UNIT) + u] for u in range(CHUNK // UNIT)], axis=1)

        def group(g, carry):
            for h in range(CHUNK // 2):
                pair = g * (CHUNK // 2) + h
                weights = jnp.concatenate(
                    [
                        jnp.concatenate(
                            [tab[indices[shift + 2 * pair + t, c * CHUNK + b]] for t in (0, 1)],
                            axis=1,
                        )
                        for b in range(CHUNK)
                    ],
                    axis=0,
                )
                acc[pair] += jnp.dot(left, weights, preferred_element_type=jnp.float32)
            return carry

        lax.fori_loop(first, last, group, 0)

    send_index.wait()

    @pl.when(has_out)
    def _():
        pass_index.start()

    to_mate = pltpu.make_async_copy(index_mate, index_mate_s, tsem.at[1])
    to_mate.start()
    to_mate.wait()

    per = CHUNK // UNIT

    def far_part(c):
        for u in range(per):
            pass_source(c * per + u).wait_recv()
        multiply(far, index_far_s, c, 2 * owned * (1 - odd), odd * c, jnp.where(odd == 1, chunks, c + 1))

    def relay(u):
        send_source(u).wait_recv()

        @pl.when(has_out)
        def _():
            pass_source(u).start()

    def work(c, carry):
        for u in range(per // 2):
            relay(c * per + u)
        multiply(source, index_smem, c, owned, 0, chunks)
        for u in range(per // 2, per):
            relay(c * per + u)
        multiply(mate, index_mate_s, c, 2 * owned * odd, (1 - odd) * c, jnp.where(odd == 1, c + 1, chunks))

        @pl.when(jnp.logical_and(has_in, c == 0))
        def _():
            pass_index.wait_recv()
            to_far = pltpu.make_async_copy(index_far, index_far_s, tsem.at[2])
            to_far.start()
            to_far.wait()

        @pl.when(jnp.logical_and(has_in, c >= 1))
        def _():
            far_part(c - 1)

        return carry

    lax.fori_loop(0, chunks, work, 0)

    @pl.when(has_in)
    def _():
        far_part(chunks - 1)

    def finish(i, carry):
        for t in (0, 1):
            lanes = slice(t * width, (t + 1) * width)
            inverse = 1.0 / acc[i, points : points + 1, lanes]
            result[pl.ds(2 * i + t, rows, stride=owned)] = acc[i, :, lanes] * inverse
        return carry

    lax.fori_loop(0, owned // 2, finish, 0)

    def write(q, carry):
        for r in range(cut):
            g = q * cut + r
            out[g] = result[pl.ds(pl.multiple_of(g * owned, owned), owned)].astype(out.dtype)
        return carry

    lax.fori_loop(0, slabs, write, 0)
    for h in range(halves):
        for q in range(slabs):
            send_part(h, q).wait_send()

    def drain(u, carry):
        send_source(u).wait_send()

        @pl.when(has_out)
        def _():
            pass_source(u).wait_send()

        return carry

    lax.fori_loop(0, units, drain, 0)

    @pl.when(has_out)
    def _():
        pass_index.wait_send()


def per_device(kernels, counts, volume, tables, pair_offset, pair_table):
    events, owned = kernels.shape[0], volume.shape[1]
    points, width = kernels.shape[3:]
    rows = -(-(points + 1) // 16) * 16
    cut = points // 5 if points % 5 == 0 else points
    units = owned // UNIT
    targets = pair_offset[0, 0].T + jnp.arange(owned, dtype=jnp.int32)
    here = targets[:, None, :] == jnp.arange(3 * owned, dtype=jnp.int32)[:, None]
    index = jnp.sum(jnp.where(here, pair_table[0, 0].T[:, None, :] + 1, 0), axis=0, dtype=jnp.int32)
    index = jnp.pad(index, ((0, 0), (0, -owned % 128)))
    sizes = dict(
        dom=lax.axis_size("dom"), events=events, owned=owned, points=points, width=width,
        tables=tables.shape[0], cut=cut,
    )
    vmem = pl.BlockSpec(memory_space=pltpu.VMEM)
    hbm = pl.BlockSpec(memory_space=pl.ANY)
    dma = pltpu.SemaphoreType.DMA
    bf16, f32, i32 = jnp.bfloat16, jnp.float32, jnp.int32
    blocks = pltpu.VMEM((units, rows, UNIT * width), bf16)
    part = pltpu.VMEM((owned // HALF, points // cut, cut, HALF, width), bf16)
    pairs = (3 * owned, index.shape[1])
    result = pl.pallas_call(
        functools.partial(kernel, sizes),
        out_shape=jax.ShapeDtypeStruct((points, owned, width), bf16),
        in_specs=[hbm, vmem, vmem, hbm, pl.BlockSpec(memory_space=pltpu.SMEM), vmem],
        out_specs=vmem,
        scratch_shapes=[
            pltpu.VMEM((2, owned // HALF, events, points, HALF, width), bf16),
            part, part,
            pltpu.VMEM((owned, width), i32),
            pltpu.VMEM((owned, width), i32),
            pltpu.VMEM((rows * HALF, width), f32),
            pltpu.VMEM((rows * owned, width), f32),
            blocks, blocks, blocks,
            pltpu.VMEM((tables.shape[0] + 1, width, width), bf16),
            pltpu.VMEM((owned // 2, rows, 2 * width), f32),
            pltpu.VMEM(pairs, i32),
            pltpu.VMEM(pairs, i32),
            pltpu.SMEM(pairs, i32),
            pltpu.SMEM(pairs, i32),
            dma((2, owned // HALF)),
            dma((3,)),
            dma((2, 1)),
            dma((2, owned // HALF, points // cut)),
            dma((2, 2)),
            dma((2, units)),
            dma((2, units)),
        ],
        compiler_params=pltpu.CompilerParams(
            collective_id=0, has_side_effects=True, vmem_limit_bytes=60 * 2**20
        ),
    )(kernels.transpose(0, 1, 3, 2, 4), counts, volume, tables, index, index)
    return result.transpose(1, 0, 2)[None]


def solution(mesh):
    in_specs = (
        P("event", "dom", None, None, None),
        P("event", "dom", None, None),
        P("dom", "event", None),
        P(),
        P("dom", "event", None, None),
        P("dom", "event", None, None),
    )
    out_specs = P("dom", "event", None, None)
    return jax.shard_map(
        per_device, mesh=mesh, in_specs=in_specs, out_specs=out_specs, check_vma=False
    )
```

time: 54.5 us -> 46.6 us (0.86)
  Pallas kernels: 45.8 us -> 41.6 us
  local copies, waits for them, and re-layouts: 6.6 us -> 2.96 us
    pallas_call x1, Pallas kernels: 45.8 us -> 41.6 us  [per_device(): pl.pallas_call(functools.partial(kernel, sizes), out_shape=jax.ShapeDtype...]
    unnamed x7 -> x1, local copies, waits for them, and re-layouts: 4.82 us -> 2.24 us
    broadcast_in_dim x1 -> x0, local copies, waits for them, and re-layouts: 1.62 us -> none  [per_device(): pl.pallas_call(functools.partial(kernel, sizes), out_shape=jax.ShapeDtype...]
    pad x0 -> x1, local copies, waits for them, and re-layouts: none -> 0.63 us  [per_device(): index = jnp.pad(index, ((0, 0), (0, -owned % 128)))]
where the time goes in v2:
time: 46.6 us; the launch traced here: 46.2 us
  Pallas kernels  41.6 us (89%)
  local copies, waits for them, and re-layouts  2.96 us (6%)
  other arithmetic  1.6 us (3%)
    pallas_call x1, Pallas kernels, per_device(): pl.pallas_call(functools.partial(kernel, sizes), out_shape=jax.ShapeDtype...  41.6 us
    unnamed x1, local copies, waits for them, and re-layouts  2.24 us

profile of v2, /device:TPU:8, one launch (start us, length us, event | category | flops | bytes accessed | tf_op | source)
XLA Modules:
  0.0 46.2 jit_solution(17494052447089011882)
XLA Ops:
  0.0 0.7 %bitcast_add_fusion = s32[16,32]{1,0:T(8,128)S(1)} fusion(s32[1,1,32,16]{2,3,1,0:T(8,128)} %param.10), kind=kLoop, calls=%fused_computation.2 | loop fusion | flops 512 | bytes 4096 | tf_op jit(solution)/shard_map/add | solution.py:246
  0.7 0.7 %add_bitcast_fusion = s32[16,32]{1,0:T(8,128)S(1)} fusion(s32[1,1,32,16]{2,3,1,0:T(8,128)} %param.11), kind=kLoop, calls=%fused_computation.3 | loop fusion | flops 512 | bytes 4096 | tf_op jit(solution)/shard_map/add | solution.py:248
  1.4 0.2 select_reduce_fusion
  1.6 0.1 copy.7
  1.7 0.6 %pad.4.index_smem.index_vmem = s32[96,128]{1,0:T(8,128)} pad(s32[96,32]{1,0:T(8,128)S(1)} %copy.7, s32[]{:T(128)} %constant.1.clone.1), padding=0_0x0_96 | pad | bytes 61444 | tf_op jit(solution)/shard_map/jit(_pad)/pad | solution.py:249
  2.3 41.6 %shard_map.64 = bf16[125,32,128]{2,1,0:T(8,128)(2,1)} custom-call(bf16[2,1,125,64,128]{4,3,2,1,0:T(8,128)(2,1)} %bitcast.13, s32[2,1,64,128]{3,2,1,0:T(8,128)} %counts.1, bf16[1,32,128]{2,1,0:T(8,128)(2,1)} %volume.1, bf16[32,128,128]{2,1,0:T(8,128)(2,1)} %tables.1, s32[96,128]{1,0:T(8,128)} %pad.4.index_smem.index_vmem, s32[96,128]{1,0:T(8,128)} %pad.4.index_smem.index_vmem), custom_call_target="tpu_custom_call" | custom-call | tf_op jit(solution)/shard_map/pallas_call | solution.py:261
  44.0 2.2 %copy.9 = bf16[1,32,125,128]{3,1,2,0:T(8,128)(2,1)} copy(bf16[1,32,125,128]{3,1,2,0:T(8,128)(2,1)} %bitcast.12) | data formatting | bytes 2048000

commit v3 on v2

--- a/solution.py
+++ b/solution.py
@@ -15,9 +15,9 @@
 
 def kernel(
     sizes,
-    kernels, counts, volume, tables, index_smem, index_vmem, out,
+    kernels, counts, volume, tables, offsets, names, out,
     kbuf, part_out, part_in, count_out, count_in, stage, result,
-    source, mate, far, tab, acc, index_mate, index_far, index_mate_s, index_far_s,
+    source, mate, far, tab, acc, index_own, index_smem, index_mate, index_far, index_mate_s, index_far_s,
     ksem, tsem, csem, xsem, isem, msem, fsem,
 ):
     n = sizes["dom"]
@@ -48,6 +48,18 @@
     get_tables = pltpu.make_async_copy(tables, tab.at[pl.ds(1, sizes["tables"])], tsem.at[0])
     get_tables.start()
 
+    group = width // owned
+    spread = lambda value: jnp.concatenate([value] * group, axis=1)
+    targets = spread(offsets[...] + lax.broadcasted_iota(jnp.int32, offsets.shape, 1))
+    found = spread(names[...] + 1)
+    places = lax.broadcasted_iota(jnp.int32, index_own.shape, 0) * group
+    places = places + lax.broadcasted_iota(jnp.int32, index_own.shape, 1) // owned
+    index = jnp.zeros(index_own.shape, jnp.int32)
+    for k in range(offsets.shape[0]):
+        index = jnp.where(targets[k : k + 1] == places, found[k : k + 1], index)
+    index_own[...] = index
+    third = owned // group
+
     barrier = pltpu.get_barrier_semaphore()
     pl.semaphore_signal(barrier, inc=1, device_id=buddy, device_id_type=MESH)
     pl.semaphore_signal(barrier, inc=1, device_id=partner, device_id_type=MESH)
@@ -76,12 +88,14 @@
         )
 
     send_count = remote(count_out, count_in, csem, (0,), buddy)
-    send_index = remote(index_vmem, index_mate, isem, (0,), partner)
+    send_index = remote(index_own, index_mate, isem, (0,), partner)
     pass_index = remote(index_mate, index_far, isem, (1,), far_out)
     send_part = lambda h, q: remote(part_out.at[h, q], part_in.at[h, q], xsem, (h, q), buddy)
     send_source = lambda u: remote(source.at[u], mate.at[u], msem, (u,), partner)
     pass_source = lambda u: remote(mate.at[u], far.at[u], fsem, (u,), far_out)
     send_count.start()
+    to_own = pltpu.make_async_copy(index_own.at[pl.ds(third, third)], index_smem, tsem.at[3])
+    to_own.start()
     send_index.start()
 
     def event_sum(side, h, g):
@@ -128,18 +142,21 @@
             send_source(unit).start()
 
     get_tables.wait()
-
-    def multiply(blocks, indices, c, shift, first, last):
+    to_own.wait()
+
+    def multiply(blocks, indices, c, first, last):
         left = jnp.concatenate([blocks[c * (CHUNK // UNIT) + u] for u in range(CHUNK // UNIT)], axis=1)
 
-        def group(g, carry):
+        def name(g, at, b):
+            return indices[g * (CHUNK // group) + at // group, at % group * owned + c * CHUNK + b]
+
+        def targets_of(g, carry):
             for h in range(CHUNK // 2):
                 pair = g * (CHUNK // 2) + h
                 weights = jnp.concatenate(
                     [
                         jnp.concatenate(
-                            [tab[indices[shift + 2 * pair + t, c * CHUNK + b]] for t in (0, 1)],
-                            axis=1,
+                            [tab[name(g, 2 * h + t, b)] for t in (0, 1)], axis=1
                         )
                         for b in range(CHUNK)
                     ],
@@ -148,7 +165,7 @@
                 acc[pair] += jnp.dot(left, weights, preferred_element_type=jnp.float32)
             return carry
 
-        lax.fori_loop(first, last, group, 0)
+        lax.fori_loop(first, last, targets_of, 0)
 
     send_index.wait()
 
@@ -156,7 +173,9 @@
     def _():
         pass_index.start()
 
-    to_mate = pltpu.make_async_copy(index_mate, index_mate_s, tsem.at[1])
+    to_mate = pltpu.make_async_copy(
+        index_mate.at[pl.ds(pl.multiple_of(2 * third * odd, third), third)], index_mate_s, tsem.at[1]
+    )
     to_mate.start()
     to_mate.wait()
 
@@ -165,7 +184,7 @@
     def far_part(c):
         for u in range(per):
             pass_source(c * per + u).wait_recv()
-        multiply(far, index_far_s, c, 2 * owned * (1 - odd), odd * c, jnp.where(odd == 1, chunks, c + 1))
+        multiply(far, index_far_s, c, odd * c, jnp.where(odd == 1, chunks, c + 1))
 
     def relay(u):
         send_source(u).wait_recv()
@@ -177,15 +196,18 @@
     def work(c, carry):
         for u in range(per // 2):
             relay(c * per + u)
-        multiply(source, index_smem, c, owned, 0, chunks)
+        multiply(source, index_smem, c, 0, chunks)
         for u in range(per // 2, per):
             relay(c * per + u)
-        multiply(mate, index_mate_s, c, 2 * owned * odd, (1 - odd) * c, jnp.where(odd == 1, c + 1, chunks))
+        multiply(mate, index_mate_s, c, (1 - odd) * c, jnp.where(odd == 1, c + 1, chunks))
 
         @pl.when(jnp.logical_and(has_in, c == 0))
         def _():
             pass_index.wait_recv()
-            to_far = pltpu.make_async_copy(index_far, index_far_s, tsem.at[2])
+            to_far = pltpu.make_async_copy(
+                index_far.at[pl.ds(pl.multiple_of(2 * third * (1 - odd), third), third)],
+                index_far_s, tsem.at[2],
+            )
             to_far.start()
             to_far.wait()
 
@@ -243,10 +265,6 @@
     rows = -(-(points + 1) // 16) * 16
     cut = points // 5 if points % 5 == 0 else points
     units = owned // UNIT
-    targets = pair_offset[0, 0].T + jnp.arange(owned, dtype=jnp.int32)
-    here = targets[:, None, :] == jnp.arange(3 * owned, dtype=jnp.int32)[:, None]
-    index = jnp.sum(jnp.where(here, pair_table[0, 0].T[:, None, :] + 1, 0), axis=0, dtype=jnp.int32)
-    index = jnp.pad(index, ((0, 0), (0, -owned % 128)))
     sizes = dict(
         dom=lax.axis_size("dom"), events=events, owned=owned, points=points, width=width,
         tables=tables.shape[0], cut=cut,
@@ -257,11 +275,12 @@
     bf16, f32, i32 = jnp.bfloat16, jnp.float32, jnp.int32
     blocks = pltpu.VMEM((units, rows, UNIT * width), bf16)
     part = pltpu.VMEM((owned // HALF, points // cut, cut, HALF, width), bf16)
-    pairs = (3 * owned, index.shape[1])
+    pairs = (3 * owned * owned // width, width)
+    third = pltpu.SMEM((owned * owned // width, width), i32)
     result = pl.pallas_call(
         functools.partial(kernel, sizes),
         out_shape=jax.ShapeDtypeStruct((points, owned, width), bf16),
-        in_specs=[hbm, vmem, vmem, hbm, pl.BlockSpec(memory_space=pltpu.SMEM), vmem],
+        in_specs=[hbm, vmem, vmem, hbm, vmem, vmem],
         out_specs=vmem,
         scratch_shapes=[
             pltpu.VMEM((2, owned // HALF, events, points, HALF, width), bf16),
@@ -274,11 +293,13 @@
             pltpu.VMEM((tables.shape[0] + 1, width, width), bf16),
             pltpu.VMEM((owned // 2, rows, 2 * width), f32),
             pltpu.VMEM(pairs, i32),
+            third,
             pltpu.VMEM(pairs, i32),
-            pltpu.SMEM(pairs, i32),
-            pltpu.SMEM(pairs, i32),
+            pltpu.VMEM(pairs, i32),
+            third,
+            third,
             dma((2, owned // HALF)),
-            dma((3,)),
+            dma((4,)),
             dma((2, 1)),
             dma((2, owned // HALF, points // cut)),
             dma((2, 2)),
@@ -288,7 +309,7 @@
         compiler_params=pltpu.CompilerParams(
             collective_id=0, has_side_effects=True, vmem_limit_bytes=60 * 2**20
         ),
-    )(kernels.transpose(0, 1, 3, 2, 4), counts, volume, tables, index, index)
+    )(kernels.transpose(0, 1, 3, 2, 4), counts, volume, tables, pair_offset[0, 0].T, pair_table[0, 0].T)
     return result.transpose(1, 0, 2)[None]
 
 

time: 46.6 us -> 42.7 us (0.916)
  other arithmetic: 1.6 us -> 0 us
  Pallas kernels: 41.6 us -> 40.3 us
  local copies, waits for them, and re-layouts: 2.96 us -> 2.24 us
    add x2 -> x0, other arithmetic: 1.4 us -> none  [the longest x1 0.7 us: per_device(): targets = pair_offset[0, 0].T + jnp.arange(owned, dtype=jnp.int32)]
    pallas_call x1, Pallas kernels: 41.6 us -> 40.3 us  [per_device(): pl.pallas_call(functools.partial(kernel, sizes), out_shape=jax.ShapeDtype...]
    pad x1 -> x0, local copies, waits for them, and re-layouts: 0.63 us -> none  [per_device(): index = jnp.pad(index, ((0, 0), (0, -owned % 128)))]
where the time goes in v3:
time: 42.7 us; the launch traced here: 42.5 us
  Pallas kernels  40.3 us (94%)
  local copies, waits for them, and re-layouts  2.24 us (5%)
    pallas_call x1, Pallas kernels, per_device(): pl.pallas_call(functools.partial(kernel, sizes), out_shape=jax.ShapeDtype...  40.3 us
    unnamed x1, local copies, waits for them, and re-layouts  2.24 us

profile of v3, /device:TPU:8, one launch (start us, length us, event | category | flops | bytes accessed | tf_op | source)
XLA Modules:
  0.0 42.5 jit_solution(5295060343097779503)
XLA Ops:
  0.0 40.3 %shard_map.64 = bf16[125,32,128]{2,1,0:T(8,128)(2,1)} custom-call(bf16[2,1,125,64,128]{4,3,2,1,0:T(8,128)(2,1)} %bitcast.10, s32[2,1,64,128]{3,2,1,0:T(8,128)} %counts.1, bf16[1,32,128]{2,1,0:T(8,128)(2,1)} %volume.1, bf16[32,128,128]{2,1,0:T(8,128)(2,1)} %tables.1, s32[16,32]{1,0:T(8,128)} %bitcast.12, s32[16,32]{1,0:T(8,128)} %bitcast.13), custom_call_target="tpu_custom_call" | custom-call | tf_op jit(solution)/shard_map/pallas_call | solution.py:280
  40.3 2.2 %copy.8 = bf16[1,32,125,128]{3,1,2,0:T(8,128)(2,1)} copy(bf16[1,32,125,128]{3,1,2,0:T(8,128)(2,1)} %bitcast.11) | data formatting | bytes 2048000
